TPU v7x, 32 devices: a whole 2x2x4 slice. The times are simulated.
32 devices in a mesh: groups: 2 (over y), pipe: 4 (over z), hour: 2 (over x), seg: 2 (over core).
Axes of the slice: x: 2, y: 2, z: 4, core: 2. Of those that a mesh axis runs over, the one named last changes fastest.
Arguments:
- segment_flow: float32 [16, 64, 1024], P(('groups', 'hour'), 'seg', 'pipe'), parts along dimension 0, may hold values from -4 to 4
- linepack: float32 [16, 64, 1024], P(('groups', 'hour'), 'seg', 'pipe'), parts along dimension 0, may hold values from 0.2 to 2.4
- mass_dual: float32 [16, 64, 1024], P(('groups', 'hour'), 'seg', 'pipe'), parts along dimension 0, may hold values from -3 to 3
- momentum_dual: float32 [16, 64, 1024], P(('groups', 'hour'), 'seg', 'pipe'), parts along dimension 0, may hold values from -3 to 3
- contract_dual: float32 [16, 2, 32, 128], P(('groups', 'hour'), 'seg', 'pipe'), parts along dimension 0, may hold values from -3 to 3
- flow_cost: float32 [16, 64, 1024], P(('groups', 'hour'), 'seg', 'pipe'), parts along dimension 0, may hold values from -24 to 24
- injection: float32 [16, 64, 1024], P(('groups', 'hour'), 'seg', 'pipe'), parts along dimension 0, may hold values from -3 to 3
- contract_target: float32 [16, 2, 32, 128], P(('groups', 'hour'), 'seg', 'pipe'), parts along dimension 0, may hold values from 0.4 to 2
- friction_table: float32 [16], replicated, may hold values from 0.3 to 3
- friction_class: int32 [64, 2048], P('seg', ('groups', 'pipe')), parts along dimension 1, may hold values from 0 to 15
- matching: int32 [2048], P('groups'), parts along dimension 0, may hold values from 0 to 1023, as said below
- contract_map: int32 [16, 1024], P(('groups', 'hour')), parts along dimension 0, may hold values from 0 to 127
Outputs:
- flow_final: float32 [16, 64, 1024], P(('groups', 'hour'), 'seg', 'pipe'), parts along dimension 0
- linepack_final: float32 [16, 64, 1024], P(('groups', 'hour'), 'seg', 'pipe'), parts along dimension 0
- mass_dual_final: float32 [16, 64, 1024], P(('groups', 'hour'), 'seg', 'pipe'), parts along dimension 0
- momentum_dual_final: float32 [16, 64, 1024], P(('groups', 'hour'), 'seg', 'pipe'), parts along dimension 0
- contract_dual_final: float32 [16, 2, 32, 128], P(('groups', 'hour'), 'seg', 'pipe'), parts along dimension 0
- primal_weight: float32 [2], P('groups'), parts along dimension 0
There are 2 independent parts, one for each index of `groups`. A program takes and returns all parts, laid end to end along the dimension named above; an argument that names none is the same for every part. Nothing has to cross between parts.
Inputs may be any that keep to these rules, and one draw needn't show every extreme that they name: `matching`: every pipe's inlet is fed by the outlet of exactly one pipe: each number of 0 to 1023 appears once; for any two blocks of 256 consecutive pipes, exactly 64 pipes of the first are fed from outlets of the second.
All inputs are finite; a program needn't handle non-finite values.
Results may differ from a plain program's by a relative error of at most 0.0001.
Values sent between devices are 32-bit elements; how exact they have to be, the bound alone decides.
A program may use at most 64 MiB of HBM per device.

v0:
```python
import math

import jax
import jax.numpy as jnp
from jax import lax
from jax.sharding import PartitionSpec as P

ITERS = 2


FLOW_CAP = 1.5
PACK_CAP = 2.5
STEP_SCALE = 0.25
NORM_EPS = 1e-06


def padded(cells, sides, width):
    for axis, dim in sides:
        count = lax.axis_size(axis)
        ends = count - 1
        head = lax.slice_in_dim(cells, 0, width, axis=dim)
        tail = lax.slice_in_dim(cells, cells.shape[dim] - width, cells.shape[dim], axis=dim)
        cells = jnp.concatenate(
            [
                lax.ppermute(tail, axis, [(i, (i + 1) % count) for i in range(ends)]),
                cells,
                lax.ppermute(head, axis, [((i + 1) % count, i) for i in range(ends)]),
            ],
            axis=dim,
        )
    return cells


def widened_pair(stacked):
    return padded(stacked, (("hour", 1), ("seg", 2)), 1)


def other_half(edge_row, half_index, partner_local):
    gathered = lax.all_gather(edge_row[:, None, :], ("pipe", "seg"), axis=1, tiled=True)
    hour_rows, row_count, row_width = gathered.shape
    seg_count = lax.axis_size("seg")
    picked = gathered.reshape(hour_rows, row_count // seg_count, seg_count, row_width)[
        :, :, half_index, :
    ]
    far_rows = picked.reshape(hour_rows, row_count // seg_count * row_width)
    return jnp.take(far_rows, partner_local, axis=1)


def contract_local(values, contract_rows, class_count):
    hour_rows, seg_rows, pipe_rows = values.shape
    block = math.gcd(pipe_rows, 2048)
    classes = jnp.arange(class_count, dtype=jnp.int32)

    def add_block(block_index, total):
        partial_value = lax.dynamic_slice_in_dim(values, block_index * block, block, 2)
        row_map = lax.dynamic_slice_in_dim(contract_rows, block_index * block, block, 1)
        onehot = (row_map[:, :, None] == classes[None, None, :]).astype(jnp.float32)
        return total + jnp.einsum(
            "hsp,hpc->hsc",
            partial_value,
            onehot,
            precision=lax.Precision.HIGHEST,
            preferred_element_type=jnp.float32,
        )

    return lax.fori_loop(
        0, pipe_rows // block, add_block, jnp.zeros((hour_rows, seg_rows, class_count), jnp.float32)
    )


def spread_local(duals, contract_rows):
    hour_rows, seg_rows, class_count = duals.shape
    pipe_rows = contract_rows.shape[1]
    block = math.gcd(pipe_rows, 2048)
    classes = jnp.arange(class_count, dtype=jnp.int32)

    def fill_block(block_index, result_now):
        row_map = lax.dynamic_slice_in_dim(contract_rows, block_index * block, block, 1)
        onehot = (row_map[:, :, None] == classes[None, None, :]).astype(jnp.float32)
        partial_value = jnp.einsum(
            "hsc,hpc->hsp",
            duals,
            onehot,
            precision=lax.Precision.HIGHEST,
            preferred_element_type=jnp.float32,
        )
        return lax.dynamic_update_slice_in_dim(result_now, partial_value, block_index * block, 2)

    return lax.fori_loop(
        0, pipe_rows // block, fill_block, jnp.zeros((hour_rows, seg_rows, pipe_rows), jnp.float32)
    )


def on_device(
    segment_flow,
    linepack,
    mass_dual,
    momentum_dual,
    contract_dual,
    flow_cost,
    injection,
    contract_target,
    friction_table,
    friction_class,
    matching,
    contract_map,
):
    hour_rows, seg_rows, pipe_rows = segment_flow.shape
    class_count = contract_dual.shape[3]
    pipe_count = lax.axis_size("pipe")
    total_pipes = pipe_rows * pipe_count
    share_scale = class_count / total_pipes
    pipe_start = lax.axis_index("pipe") * pipe_rows
    seg_index = lax.axis_index("seg")
    at_start = seg_index == 0
    at_end = seg_index == lax.axis_size("seg") - 1
    levels = jnp.arange(friction_table.shape[0], dtype=jnp.int32)
    friction = jnp.sum(
        jnp.where(
            friction_class[None] == levels[:, None, None], friction_table[:, None, None], 0.0
        ),
        axis=0,
    )[None]
    inverse = (
        jnp.zeros_like(matching).at[matching].set(jnp.arange(matching.shape[0], dtype=jnp.int32))
    )
    source_local = lax.dynamic_slice_in_dim(matching, pipe_start, pipe_rows)
    target_local = lax.dynamic_slice_in_dim(inverse, pipe_start, pipe_rows)
    contract_now = contract_dual.reshape(hour_rows, contract_dual.shape[2], class_count)
    target_now = contract_target.reshape(hour_rows, contract_target.shape[2], class_count)
    weight = jnp.float32(1.0)
    for iteration in range(ITERS):
        primal_step = STEP_SCALE / weight
        dual_step = STEP_SCALE * weight
        widened = widened_pair(jnp.stack([mass_dual, momentum_dual]))
        last_base = widened[0, 1:-1, -1, :]
        later_hour = widened[0, 2:, 1:-1, :]
        before_seg = widened[1, 1:-1, :-2, :]
        returned = other_half(mass_dual[:, 0, :], 0, target_local)
        last_row = last_base + jnp.where(at_end, returned, 0.0)
        next_seg = jnp.concatenate([mass_dual[:, 1:, :], last_row[:, None, :]], axis=1)
        grad_flow = mass_dual - next_seg + friction * momentum_dual
        hour_spread = spread_local(contract_now, contract_map)
        spread = lax.all_to_all(hour_spread, "pipe", split_axis=2, concat_axis=1, tiled=True)
        grad_pack = mass_dual - later_hour - momentum_dual + before_seg + share_scale * spread
        grad_flow, grad_pack = (grad_flow, grad_pack)
        flow_next = jnp.clip(
            segment_flow - primal_step * (flow_cost - grad_flow), -FLOW_CAP, FLOW_CAP
        )
        pack_next = jnp.clip(linepack + primal_step * grad_pack, 0.0, PACK_CAP)
        flow_bar = 2.0 * flow_next - segment_flow
        pack_bar = 2.0 * pack_next - linepack
        forward_widened = widened_pair(jnp.stack([flow_bar, pack_bar]))
        first_base = forward_widened[0, 1:-1, 0, :]
        earlier = forward_widened[1, :-2, 1:-1, :]
        after_seg = forward_widened[1, 1:-1, 2:, :]
        inflow = other_half(flow_bar[:, -1, :], 1, source_local)
        first_row = first_base + jnp.where(at_start, inflow, 0.0)
        upstream = jnp.concatenate([first_row[:, None, :], flow_bar[:, :-1, :]], axis=1)
        mass_rows = pack_bar - earlier + flow_bar - upstream
        momentum = friction * flow_bar - (pack_bar - after_seg)
        hour_major = lax.all_to_all(pack_bar, "pipe", split_axis=1, concat_axis=2, tiled=True)
        totals = contract_local(hour_major, contract_map, class_count)
        mass_rows, momentum, totals = (mass_rows, momentum, share_scale * totals)
        mass_next = mass_dual + dual_step * (injection - mass_rows)
        momentum_next = momentum_dual - dual_step * momentum
        contract_next = contract_now + dual_step * (target_now - totals)
        primal_sq = jnp.sum((flow_next - segment_flow) ** 2) + jnp.sum((pack_next - linepack) ** 2)
        dual_sq = (
            jnp.sum((mass_next - mass_dual) ** 2)
            + jnp.sum((momentum_next - momentum_dual) ** 2)
            + jnp.sum((contract_next - contract_now) ** 2)
        )
        primal_total, dual_total = lax.psum((primal_sq, dual_sq), ("pipe", "hour", "seg"))
        weight = jnp.sqrt(weight * jnp.sqrt((dual_total + NORM_EPS) / (primal_total + NORM_EPS)))
        segment_flow, linepack = (flow_next, pack_next)
        mass_dual, momentum_dual, contract_now = (mass_next, momentum_next, contract_next)
    return (
        segment_flow,
        linepack,
        mass_dual,
        momentum_dual,
        contract_now.reshape(contract_dual.shape),
        weight.reshape(1),
    )


def solution(mesh):
    return jax.shard_map(
        on_device,
        mesh=mesh,
        in_specs=(
            P(("groups", "hour"), "seg", "pipe"),
            P(("groups", "hour"), "seg", "pipe"),
            P(("groups", "hour"), "seg", "pipe"),
            P(("groups", "hour"), "seg", "pipe"),
            P(("groups", "hour"), "seg", "pipe", None),
            P(("groups", "hour"), "seg", "pipe"),
            P(("groups", "hour"), "seg", "pipe"),
            P(("groups", "hour"), "seg", "pipe", None),
            P(),
            P("seg", ("groups", "pipe")),
            P("groups"),
            P(("groups", "hour"), None),
        ),
        out_specs=(
            P(("groups", "hour"), "seg", "pipe"),
            P(("groups", "hour"), "seg", "pipe"),
            P(("groups", "hour"), "seg", "pipe"),
            P(("groups", "hour"), "seg", "pipe"),
            P(("groups", "hour"), "seg", "pipe", None),
            P("groups"),
        ),
        check_vma=False,
    )
```

profile of v0, /device:TPU:0, one launch (start us, length us, event | category | flops | bytes accessed | tf_op | source)
XLA Modules:
  0.0 255.9 jit_solution(9958504613072737630)
XLA Ops:
  0.6 2.2 fusion.4
  3.7 3.1 %reshape.116 = f32[4,1,8192]{2,1,0:T(1,128)} reshape(f32[1024,4,8]{2,1,0:T(4,128)S(1)} %bitcast.195) | data formatting | bytes 262144
  6.8 6.3 %all-to-all-start = ((f32[4,1,8192]{2,1,0:T(1,128)}), f32[4,1,8192]{2,1,0:T(1,128)S(1)}, u32[]{:S(2)}, u32[]{:S(2)}) async-start(f32[4,1,8192]{2,1,0:T(1,128)} %reshape.116), calls=%async_computation | async-start | bytes 262144 | tf_op jit(solution)/shard_map/all_to_all | solution.py:144
  14.5 4.5 %collective-permute-start = (f32[2,1,32,256]{3,2,1,0:T(8,128)S(1)}, f32[2,1,32,256]{3,2,1,0:T(8,128)S(1)}, u32[]{:S(2)}, u32[]{:S(2)}) collective-permute-start(f32[2,1,32,256]{3,2,1,0:T(8,128)S(1)} %get-tuple-element.135), channel_id=1, source_target_pairs={{0,2},{1,3},{4,6},{5,7},{8,10},{9,11},{12,14},{13,15},{16,18},{17,... | collective-permute-start | bytes 196616 | tf_op jit(solution)/shard_map/ppermute | solution.py:25
  19.1 14.6 %all_gather.12 = f32[4,8,256]{2,0,1:T(4,128)S(1)} all-gather(f32[4,1,256]{2,0,1:T(4,128)S(1)} %copy.255), channel_id=1, replica_groups=mesh['groups'=2,'pipe'=4,'hour'=2,'seg'=2] {'pipe','seg'}, dimensions={1}, use_global_device_ids=true | all-gather | bytes 36864 | tf_op jit(solution)/shard_map/all_gather | solution.py:39
  33.9 4.3 %scatter_custom_fusion = s32[1024]{0:T(1024)S(1)} fusion(s32[1024]{0:T(1024)S(1)} %compare_select_fusion, s32[1024]{0:T(1024)S(1)} %iota.14, s32[]{:T(128)} %constant.26.clone.1), kind=kCustom, calls=%fused_computation.140 | custom fusion | bytes 4100 | tf_op jit(solution)/shard_map/scatter | solution.py:125
  40.3 2.2 collective-permute-start.3
  47.8 2.5 reshape.117
  50.4 1.8 broadcast_multiply_fusion.1
  52.2 1.9 copy.145
  58.7 4.5 %collective-permute-start.4 = (f32[2,1,32,256]{3,2,1,0:T(8,128)S(1)}, f32[2,1,32,256]{3,2,1,0:T(8,128)S(1)}, u32[]{:S(2)}, u32[]{:S(2)}) collective-permute-start(f32[2,1,32,256]{3,2,1,0:T(8,128)S(1)} %get-tuple-element.131), channel_id=1, source_target_pairs={{0,2},{1,3},{4,6},{5,7},{8,10},{9,11},{12,14},{13,15},{16,18},{17,... | collective-permute-start | bytes 196616 | tf_op jit(solution)/shard_map/ppermute | solution.py:25
  63.3 14.0 %all_gather.13 = f32[4,8,256]{2,0,1:T(4,128)S(1)} all-gather(f32[4,1,256]{2,0,1:T(4,128)S(1)} %slice.182), channel_id=1, replica_groups=mesh['groups'=2,'pipe'=4,'hour'=2,'seg'=2] {'pipe','seg'}, dimensions={1}, use_global_device_ids=true | all-gather | bytes 36864 | tf_op jit(solution)/shard_map/all_gather | solution.py:39
  78.7 2.2 collective-permute-start.6
  84.0 2.0 multiply_reduce_fusion.7
  87.5 4.5 %collective-permute-start.8 = (f32[2,1,32,256]{3,2,1,0:T(8,128)S(1)}, f32[2,1,32,256]{3,2,1,0:T(8,128)S(1)}, u32[]{:S(2)}, u32[]{:S(2)}) collective-permute-start(f32[2,1,32,256]{3,2,1,0:T(8,128)S(1)} %get-tuple-element.127), channel_id=1, source_target_pairs={{0,2},{1,3},{4,6},{5,7},{8,10},{9,11},{12,14},{13,15},{16,18},{17,... | collective-permute-start | bytes 196616 | tf_op jit(solution)/shard_map/ppermute | solution.py:25
  92.0 4.5 %all-to-all-start.1 = ((f32[4,32,256]{2,0,1:T(4,128)}), f32[4,32,256]{2,0,1:T(4,128)S(1)}, u32[]{:S(2)}, u32[]{:S(2)}) async-start(f32[4,32,256]{2,0,1:T(4,128)} %multiply_subtract_fusion.3), calls=%async_computation.1 | async-start | bytes 262144 | tf_op jit(solution)/shard_map/all_to_all | solution.py:162
  98.5 14.6 %all_gather.14 = f32[4,8,256]{2,0,1:T(4,128)S(1)} all-gather(f32[4,1,256]{2,0,1:T(4,128)S(1)} %slice.191), channel_id=1, replica_groups=mesh['groups'=2,'pipe'=4,'hour'=2,'seg'=2] {'pipe','seg'}, dimensions={1}, use_global_device_ids=true | all-gather | bytes 36864 | tf_op jit(solution)/shard_map/all_gather | solution.py:39
  116.3 2.2 collective-permute-start.11
  120.7 2.2 fusion.73
  123.0 1.8 fusion.1
  125.6 3.1 %reshape.118 = f32[4,1,8192]{2,1,0:T(1,128)} reshape(f32[1024,4,8]{2,1,0:T(4,128)S(1)} %bitcast.197) | data formatting | bytes 262144
  128.7 4.5 %all-to-all-start.2 = ((f32[4,1,8192]{2,1,0:T(1,128)}), f32[4,1,8192]{2,1,0:T(1,128)S(1)}, u32[]{:S(2)}, u32[]{:S(2)}) async-start(f32[4,1,8192]{2,1,0:T(1,128)} %reshape.118), calls=%async_computation.2 | async-start | bytes 262144 | tf_op jit(solution)/shard_map/all_to_all | solution.py:144
  135.1 33.5 %all-reduce.1 = (f32[]{:T(128)}, f32[]{:T(128)}) all-reduce(f32[]{:T(128)S(6)} %add.153, f32[]{:T(128)S(6)} %add.155), channel_id=1, replica_groups=mesh['groups'=2,'pipe'=4,'hour'=2,'seg'=2] {'pipe','hour','seg'}, use_global_device_ids=true, to_apply=%region_5.7 | all-reduce | flops 2 | bytes 16 | tf_op jit(solution)/shard_map/psum | solution.py:174
  171.1 2.5 reshape.119
  175.4 1.9 copy.175
  181.3 4.5 %collective-permute-start.12 = (f32[2,1,32,256]{3,2,1,0:T(8,128)S(1)}, f32[2,1,32,256]{3,2,1,0:T(8,128)S(1)}, u32[]{:S(2)}, u32[]{:S(2)}) collective-permute-start(f32[2,1,32,256]{3,2,1,0:T(8,128)S(1)} %get-tuple-element.123), channel_id=1, source_target_pairs={{0,2},{1,3},{4,6},{5,7},{8,10},{9,11},{12,14},{13,15},{16,18},{17,... | collective-permute-start | bytes 196616 | tf_op jit(solution)/shard_map/ppermute | solution.py:25
  187.2 3.5 %all-to-all-start.3 = ((f32[4,32,256]{2,0,1:T(4,128)}), f32[4,32,256]{2,0,1:T(4,128)S(1)}, u32[]{:S(2)}, u32[]{:S(2)}) async-start(f32[4,32,256]{2,0,1:T(4,128)} %multiply_subtract_fusion.1), calls=%async_computation.3 | async-start | bytes 262144 | tf_op jit(solution)/shard_map/all_to_all | solution.py:162
  190.7 14.6 %all_gather.15 = f32[4,8,256]{2,0,1:T(4,128)S(1)} all-gather(f32[4,1,256]{2,0,1:T(4,128)S(1)} %slice.198), channel_id=1, replica_groups=mesh['groups'=2,'pipe'=4,'hour'=2,'seg'=2] {'pipe','seg'}, dimensions={1}, use_global_device_ids=true | all-gather | bytes 36864 | tf_op jit(solution)/shard_map/all_gather | solution.py:39
  209.4 3.0 %collective-permute-start.14 = (f32[2,6,1,256]{1,3,2,0:T(8,128)S(1)}, f32[2,6,1,256]{1,3,2,0:T(8,128)S(1)}, u32[]{:S(2)}, u32[]{:S(2)}) collective-permute-start(f32[2,6,1,256]{1,3,2,0:T(8,128)S(1)} %copy.201), channel_id=1, source_target_pairs={{0,1},{2,3},{4,5},{6,7},{8,9},{10,11},{12,13},{14,15},{16,17},{18,... | collective-permute-start | bytes 36872 | tf_op jit(solution)/shard_map/ppermute | solution.py:25
  213.8 1.8 multiply_reduce_fusion.2
  217.6 2.4 multiply_reduce_fusion.8
  221.4 32.0 %all-reduce = (f32[]{:T(128)}, f32[]{:T(128)}) all-reduce(f32[]{:T(128)S(6)} %add.167, f32[]{:T(128)S(6)} %add.169), channel_id=1, replica_groups=mesh['groups'=2,'pipe'=4,'hour'=2,'seg'=2] {'pipe','hour','seg'}, use_global_device_ids=true, to_apply=%region_12.14 | all-reduce | flops 2 | bytes 16 | tf_op jit(solution)/shard_map/psum | solution.py:174
  (151 shorter events, 40.3 us)
Async XLA Ops:
  2.8 10.3 %copy-start = (f32[4,32,256]{2,1,0:T(8,128)S(1)}, f32[4,32,256]{2,1,0:T(8,128)}, u32[]{:S(2)}) copy-start(f32[4,32,256]{2,1,0:T(8,128)} %param.16) | copy-start | bytes 393220
  2.8 10.3 %copy-start.1 = (f32[4,32,256]{2,1,0:T(8,128)S(1)}, f32[4,32,256]{2,1,0:T(8,128)}, u32[]{:S(2)}) copy-start(f32[4,32,256]{2,1,0:T(8,128)} %param.17) | copy-start | bytes 393220
  3.7 30.2 %copy-start.12 = (s32[1024]{0:T(1024)S(1)}, s32[1024]{0:T(1024)}, u32[]{:S(2)}) copy-start(s32[1024]{0:T(1024)} %param.24) | copy-start | bytes 12292
  3.7 35.3 %copy-start.11 = (s32[32,256]{1,0:T(8,128)S(1)}, s32[32,256]{1,0:T(8,128)}, u32[]{:S(2)}) copy-start(s32[32,256]{1,0:T(8,128)} %param.23) | copy-start | bytes 98308
  3.7 35.3 %copy-start.13 = (f32[16]{0:T(128)S(1)}, f32[16]{0:T(128)}, u32[]{:S(2)}) copy-start(f32[16]{0:T(128)} %param.22) | copy-start | bytes 196
  6.8 39.5 %all-to-all-start = ((f32[4,1,8192]{2,1,0:T(1,128)}), f32[4,1,8192]{2,1,0:T(1,128)S(1)}, u32[]{:S(2)}, u32[]{:S(2)}) async-start(f32[4,1,8192]{2,1,0:T(1,128)} %reshape.116), calls=%async_computation | async-start | bytes 262144 | tf_op jit(solution)/shard_map/all_to_all | solution.py:144
  13.2 26.8 %collective-permute-start.1 = (f32[2,1,32,256]{3,2,1,0:T(8,128)S(1)}, f32[2,1,32,256]{3,2,1,0:T(8,128)S(1)}, u32[]{:S(2)}, u32[]{:S(2)}) collective-permute-start(f32[2,1,32,256]{3,2,1,0:T(8,128)S(1)} %get-tuple-element.136), channel_id=1, source_target_pairs={{2,0},{3,1},{6,4},{7,5},{10,8},{11,9},{14,12},{15,13},{18,16},{19,... | collective-permute-start | bytes 196616 | tf_op jit(solution)/shard_map/ppermute | solution.py:27
  14.5 25.5 %collective-permute-start = (f32[2,1,32,256]{3,2,1,0:T(8,128)S(1)}, f32[2,1,32,256]{3,2,1,0:T(8,128)S(1)}, u32[]{:S(2)}, u32[]{:S(2)}) collective-permute-start(f32[2,1,32,256]{3,2,1,0:T(8,128)S(1)} %get-tuple-element.135), channel_id=1, source_target_pairs={{0,2},{1,3},{4,6},{5,7},{8,10},{9,11},{12,14},{13,15},{16,18},{17,... | collective-permute-start | bytes 196616 | tf_op jit(solution)/shard_map/ppermute | solution.py:25
  40.3 13.8 %collective-permute-start.3 = (f32[2,6,1,256]{3,1,2,0:T(8,128)S(1)}, f32[2,6,1,256]{3,1,2,0:T(8,128)S(1)}, u32[]{:S(2)}, u32[]{:S(2)}) collective-permute-start(f32[2,6,1,256]{3,1,2,0:T(8,128)S(1)} %slice.177), channel_id=1, source_target_pairs={{0,1},{2,3},{4,5},{6,7},{8,9},{10,11},{12,13},{14,15},{16,17},{18,... | collective-permute-start | bytes 36872 | tf_op jit(solution)/shard_map/ppermute | solution.py:25
  42.7 3.4 %collective-permute-start.2 = (f32[2,6,1,256]{1,3,2,0:T(8,128)S(1)}, f32[2,6,1,256]{1,3,2,0:T(8,128)S(1)}, u32[]{:S(2)}, u32[]{:S(2)}) collective-permute-start(f32[2,6,1,256]{1,3,2,0:T(8,128)S(1)} %copy.191), channel_id=1, source_target_pairs={{1,0},{3,2},{5,4},{7,6},{9,8},{11,10},{13,12},{15,14},{17,16},{19,... | collective-permute-start | bytes 36872 | tf_op jit(solution)/shard_map/ppermute | solution.py:27
  52.2 2.0 copy-start.8
  52.2 2.0 copy-start.9
  57.2 26.8 %copy-start.6 = (f32[4,32,256]{2,1,0:T(8,128)S(1)}, f32[4,32,256]{2,1,0:T(8,128)}, u32[]{:S(2)}) copy-start(f32[4,32,256]{2,1,0:T(8,128)} %param.20) | copy-start | bytes 393220
  57.2 21.0 %collective-permute-start.5 = (f32[2,1,32,256]{3,2,1,0:T(8,128)S(1)}, f32[2,1,32,256]{3,2,1,0:T(8,128)S(1)}, u32[]{:S(2)}, u32[]{:S(2)}) collective-permute-start(f32[2,1,32,256]{3,2,1,0:T(8,128)S(1)} %get-tuple-element.132), channel_id=1, source_target_pairs={{2,0},{3,1},{6,4},{7,5},{10,8},{11,9},{14,12},{15,13},{18,16},{19,... | collective-permute-start | bytes 196616 | tf_op jit(solution)/shard_map/ppermute | solution.py:27
  58.7 19.6 %collective-permute-start.4 = (f32[2,1,32,256]{3,2,1,0:T(8,128)S(1)}, f32[2,1,32,256]{3,2,1,0:T(8,128)S(1)}, u32[]{:S(2)}, u32[]{:S(2)}) collective-permute-start(f32[2,1,32,256]{3,2,1,0:T(8,128)S(1)} %get-tuple-element.131), channel_id=1, source_target_pairs={{0,2},{1,3},{4,6},{5,7},{8,10},{9,11},{12,14},{13,15},{16,18},{17,... | collective-permute-start | bytes 196616 | tf_op jit(solution)/shard_map/ppermute | solution.py:25
  78.7 3.7 %collective-permute-start.6 = (f32[2,6,1,256]{1,3,2,0:T(8,128)S(1)}, f32[2,6,1,256]{1,3,2,0:T(8,128)S(1)}, u32[]{:S(2)}, u32[]{:S(2)}) collective-permute-start(f32[2,6,1,256]{1,3,2,0:T(8,128)S(1)} %copy.195), channel_id=1, source_target_pairs={{0,1},{2,3},{4,5},{6,7},{8,9},{10,11},{12,13},{14,15},{16,17},{18,... | collective-permute-start | bytes 36872 | tf_op jit(solution)/shard_map/ppermute | solution.py:25
  81.0 3.1 %collective-permute-start.7 = (f32[2,6,1,256]{3,1,2,0:T(8,128)S(1)}, f32[2,6,1,256]{3,1,2,0:T(8,128)S(1)}, u32[]{:S(2)}, u32[]{:S(2)}) collective-permute-start(f32[2,6,1,256]{3,1,2,0:T(8,128)S(1)} %slice.185), channel_id=1, source_target_pairs={{1,0},{3,2},{5,4},{7,6},{9,8},{11,10},{13,12},{15,14},{17,16},{19,... | collective-permute-start | bytes 36872 | tf_op jit(solution)/shard_map/ppermute | solution.py:27
  86.1 34.6 %copy-start.14 = (f32[4,1,8,128]{3,2,1,0:T(8,128)S(1)}, f32[4,1,8,128]{3,2,1,0:T(8,128)}, u32[]{:S(2)}) copy-start(f32[4,1,8,128]{3,2,1,0:T(8,128)} %param.18) | copy-start | bytes 49156
  86.1 34.6 %copy-start.15 = (s32[4,1024]{1,0:T(4,128)S(1)}, s32[4,1024]{1,0:T(4,128)}, u32[]{:S(2)}) copy-start(s32[4,1024]{1,0:T(4,128)} %param.25) | copy-start | bytes 49156
  86.1 34.6 %copy-start.16 = (f32[4,1,8,128]{3,2,1,0:T(8,128)S(1)}, f32[4,1,8,128]{3,2,1,0:T(8,128)}, u32[]{:S(2)}) copy-start(f32[4,1,8,128]{3,2,1,0:T(8,128)} %param.21) | copy-start | bytes 49156
  86.2 29.8 %collective-permute-start.9 = (f32[2,1,32,256]{3,2,1,0:T(8,128)S(1)}, f32[2,1,32,256]{3,2,1,0:T(8,128)S(1)}, u32[]{:S(2)}, u32[]{:S(2)}) collective-permute-start(f32[2,1,32,256]{3,2,1,0:T(8,128)S(1)} %get-tuple-element.128), channel_id=1, source_target_pairs={{2,0},{3,1},{6,4},{7,5},{10,8},{11,9},{14,12},{15,13},{18,16},{19,... | collective-permute-start | bytes 196616 | tf_op jit(solution)/shard_map/ppermute | solution.py:27
  87.5 28.5 %collective-permute-start.8 = (f32[2,1,32,256]{3,2,1,0:T(8,128)S(1)}, f32[2,1,32,256]{3,2,1,0:T(8,128)S(1)}, u32[]{:S(2)}, u32[]{:S(2)}) collective-permute-start(f32[2,1,32,256]{3,2,1,0:T(8,128)S(1)} %get-tuple-element.127), channel_id=1, source_target_pairs={{0,2},{1,3},{4,6},{5,7},{8,10},{9,11},{12,14},{13,15},{16,18},{17,... | collective-permute-start | bytes 196616 | tf_op jit(solution)/shard_map/ppermute | solution.py:25
  92.0 28.6 %all-to-all-start.1 = ((f32[4,32,256]{2,0,1:T(4,128)}), f32[4,32,256]{2,0,1:T(4,128)S(1)}, u32[]{:S(2)}, u32[]{:S(2)}) async-start(f32[4,32,256]{2,0,1:T(4,128)} %multiply_subtract_fusion.3), calls=%async_computation.1 | async-start | bytes 262144 | tf_op jit(solution)/shard_map/all_to_all | solution.py:162
  116.3 61.0 %collective-permute-start.11 = (f32[2,6,1,256]{3,1,2,0:T(8,128)S(1)}, f32[2,6,1,256]{3,1,2,0:T(8,128)S(1)}, u32[]{:S(2)}, u32[]{:S(2)}) collective-permute-start(f32[2,6,1,256]{3,1,2,0:T(8,128)S(1)} %slice.193), channel_id=1, source_target_pairs={{0,1},{2,3},{4,5},{6,7},{8,9},{10,11},{12,13},{14,15},{16,17},{18,... | collective-permute-start | bytes 36872 | tf_op jit(solution)/shard_map/ppermute | solution.py:25
  119.3 13.9 %collective-permute-start.10 = (f32[2,6,1,256]{1,3,2,0:T(8,128)}, f32[2,6,1,256]{1,3,2,0:T(8,128)}, u32[]{:S(2)}, u32[]{:S(2)}) collective-permute-start(f32[2,6,1,256]{1,3,2,0:T(8,128)} %copy.197), channel_id=1, source_target_pairs={{1,0},{3,2},{5,4},{7,6},{9,8},{11,10},{13,12},{15,14},{17,16},{19,... | collective-permute-start | bytes 36872 | tf_op jit(solution)/shard_map/ppermute | solution.py:27
  128.7 41.3 %all-to-all-start.2 = ((f32[4,1,8192]{2,1,0:T(1,128)}), f32[4,1,8192]{2,1,0:T(1,128)S(1)}, u32[]{:S(2)}, u32[]{:S(2)}) async-start(f32[4,1,8192]{2,1,0:T(1,128)} %reshape.118), calls=%async_computation.2 | async-start | bytes 262144 | tf_op jit(solution)/shard_map/all_to_all | solution.py:144
  180.0 27.6 %collective-permute-start.13 = (f32[2,1,32,256]{3,2,1,0:T(8,128)S(1)}, f32[2,1,32,256]{3,2,1,0:T(8,128)S(1)}, u32[]{:S(2)}, u32[]{:S(2)}) collective-permute-start(f32[2,1,32,256]{3,2,1,0:T(8,128)S(1)} %get-tuple-element.124), channel_id=1, source_target_pairs={{2,0},{3,1},{6,4},{7,5},{10,8},{11,9},{14,12},{15,13},{18,16},{19,... | collective-permute-start | bytes 196616 | tf_op jit(solution)/shard_map/ppermute | solution.py:27
  181.3 26.3 %collective-permute-start.12 = (f32[2,1,32,256]{3,2,1,0:T(8,128)S(1)}, f32[2,1,32,256]{3,2,1,0:T(8,128)S(1)}, u32[]{:S(2)}, u32[]{:S(2)}) collective-permute-start(f32[2,1,32,256]{3,2,1,0:T(8,128)S(1)} %get-tuple-element.123), channel_id=1, source_target_pairs={{0,2},{1,3},{4,6},{5,7},{8,10},{9,11},{12,14},{13,15},{16,18},{17,... | collective-permute-start | bytes 196616 | tf_op jit(solution)/shard_map/ppermute | solution.py:25
  187.2 26.6 %copy-start.7 = (f32[4,32,256]{2,1,0:T(8,128)S(1)}, f32[4,32,256]{2,1,0:T(8,128)}, u32[]{:S(2)}) copy-start(f32[4,32,256]{2,1,0:T(8,128)} %param.20) | copy-start | bytes 393220
  187.2 30.4 %all-to-all-start.3 = ((f32[4,32,256]{2,0,1:T(4,128)}), f32[4,32,256]{2,0,1:T(4,128)S(1)}, u32[]{:S(2)}, u32[]{:S(2)}) async-start(f32[4,32,256]{2,0,1:T(4,128)} %multiply_subtract_fusion.1), calls=%async_computation.3 | async-start | bytes 262144 | tf_op jit(solution)/shard_map/all_to_all | solution.py:162
  207.9 5.8 %collective-permute-start.15 = (f32[2,6,1,256]{3,1,2,0:T(8,128)S(1)}, f32[2,6,1,256]{3,1,2,0:T(8,128)S(1)}, u32[]{:S(2)}, u32[]{:S(2)}) collective-permute-start(f32[2,6,1,256]{3,1,2,0:T(8,128)S(1)} %slice.201), channel_id=1, source_target_pairs={{1,0},{3,2},{5,4},{7,6},{9,8},{11,10},{13,12},{15,14},{17,16},{19,... | collective-permute-start | bytes 36872 | tf_op jit(solution)/shard_map/ppermute | solution.py:27
  209.4 4.2 %collective-permute-start.14 = (f32[2,6,1,256]{1,3,2,0:T(8,128)S(1)}, f32[2,6,1,256]{1,3,2,0:T(8,128)S(1)}, u32[]{:S(2)}, u32[]{:S(2)}) collective-permute-start(f32[2,6,1,256]{1,3,2,0:T(8,128)S(1)} %copy.201), channel_id=1, source_target_pairs={{0,1},{2,3},{4,5},{6,7},{8,9},{10,11},{12,13},{14,15},{16,17},{18,... | collective-permute-start | bytes 36872 | tf_op jit(solution)/shard_map/ppermute | solution.py:25
  (5 other events, 9.7 us)
where the time goes:
time: 257 us; the launch traced here: 256 us
  blocking collectives  123 us (48%)
  starting transfers between devices  57.3 us (22%)
  local copies, waits for them, and re-layouts  34.9 us (14%)
  other arithmetic  15.8 us (6%)
  between operations  12.1 us (5%)
  matrix products  8.66 us (3%)
  waiting for transfers between devices  3.97 us (2%)
    psum x2, blocking collectives, on_device(): lax.psum((primal_sq, dual_sq), ('pipe', 'hour', 'seg'))  65.5 us
    all_gather x4, blocking collectives, other_half(): lax.all_gather(edge_row[:, None, :], ('pipe', 'seg'), axis=1, tiled=True)  57.8 us
    ppermute x8, starting transfers between devices, padded(): lax.ppermute(tail, axis, [(i, (i + 1) % count) for i in range(ends)])  27.9 us
    unnamed x55, local copies, waits for them, and re-layouts  17 us
    all_to_all x2, starting transfers between devices, on_device(): lax.all_to_all(hour_spread, 'pipe', split_axis=2, concat_axis=1, tiled=True)  10.8 us
    ppermute x8, starting transfers between devices, padded(): lax.ppermute(head, axis, [((i + 1) % count, i) for i in range(ends)])  10.6 us
    all_to_all x2, starting transfers between devices, on_device(): lax.all_to_all(pack_bar, 'pipe', split_axis=1, concat_axis=2, tiled=True)  7.97 us
  transfers between devices with their start and end apart: 20, of which 3 were waited for; matrix products, arithmetic and copies ran while one was open for 16% of the time, Pallas kernels for 0%

commit v1 on v0

v1 whole, which is shorter than its diff:
```python
import functools

import jax
import jax.numpy as jnp
from jax import lax
from jax.experimental import pallas as pl
from jax.experimental.pallas import tpu as pltpu
from jax.sharding import PartitionSpec as P

ITERS = 2
FLOW_CAP = 1.5
PACK_CAP = 2.5
STEP_SCALE = 0.25
NORM_EPS = 1e-06
LANES = 128
PIECES = 3


def pieces_of(values):
    parts = []
    rest = values
    for _ in range(PIECES):
        part = rest.astype(jnp.bfloat16)
        rest = rest - part.astype(jnp.float32)
        parts.append(part.astype(jnp.float32))
    return jnp.concatenate(parts, axis=0).astype(jnp.bfloat16)


def joined(stacked, rows):
    total = stacked[(PIECES - 1) * rows :]
    for piece in range(PIECES - 2, -1, -1):
        total = total + stacked[piece * rows : (piece + 1) * rows]
    return total


def folded(cells):
    rows, columns = cells.shape
    total = None
    for row in range(0, rows, 8):
        for column in range(0, columns, LANES):
            block = cells[row : row + 8, column : column + LANES]
            total = block if total is None else total + block
    return total


def kernel(
    sizes,
    table_ref,
    flow_in, pack_in, mass_in, mom_in, dual_in, cost_in, inj_in, target_in, class_in, match_in, map_in,
    flow_out, pack_out, mass_out, mom_out, dual_out, weight_out,
    flow, pack, mass, mom, dual, cost, inj, target, classes, match, cmap,
    fric, flow_bar, pack_bar, onehot_c, onehot_m,
    row_send, row_recv, hour_recv, sum_send, sum_recv, dual_recv, norm_send, norm_recv,
    in_sem, out_sem, row_ss, row_rs, hour_ss, hour_rs, sum_ss, sum_rs, dual_ss, dual_rs, norm_ss, norm_rs,
):
    pipes, hours, segs, H, S, W, C, R, T = sizes
    share = C / T
    peers = pipes * hours * segs
    me_p, me_h, me_s = lax.axis_index("pipe"), lax.axis_index("hour"), lax.axis_index("seg")
    me = (me_p * hours + me_h) * segs + me_s
    other_s = lax.rem(me_s + 1, segs)
    first_half, last_half = me_s == 0, me_s == segs - 1
    first_hour, last_hour = me_h == 0, me_h == hours - 1

    def load(index, source, place):
        copy = pltpu.make_async_copy(source, place, in_sem.at[index])
        copy.start()
        return copy

    get_mass = load(0, mass_in, mass.at[0])
    get_mom = load(1, mom_in, mom.at[0])
    get_dual = load(2, dual_in, dual.at[0])
    get_match = load(3, match_in, match)
    get_map = load(4, map_in, cmap)
    get_class = load(5, class_in, classes)
    get_flow = load(6, flow_in, flow.at[0])
    get_pack = load(7, pack_in, pack.at[0])
    get_cost = load(8, cost_in, cost)
    get_inj = load(9, inj_in, inj)
    get_target = load(10, target_in, target)

    def peer(step):
        dp, rest = step // (hours * segs), step % (hours * segs)
        return {
            "pipe": lax.rem(me_p + dp, pipes),
            "hour": lax.rem(me_h + rest // segs, hours),
            "seg": lax.rem(me_s + rest % segs, segs),
        }

    def each_peer(act):
        if peers <= 32:
            for step in range(1, peers):
                act(step)
        else:
            def body(step, carry):
                act(step)
                return carry
            lax.fori_loop(1, peers, body, 0)

    barrier = pltpu.get_barrier_semaphore()

    def greet(step):
        pl.semaphore_signal(barrier, inc=1, device_id=peer(step), device_id_type=pl.DeviceIdType.MESH)

    each_peer(greet)

    sent = []

    def remote(source, place, send_sem, recv_sem, where):
        copy = pltpu.make_async_remote_copy(
            src_ref=source, dst_ref=place, send_sem=send_sem, recv_sem=recv_sem,
            device_id=where, device_id_type=pl.DeviceIdType.MESH,
        )
        copy.start()
        sent.append(copy)
        return copy

    def send_rows(turn):
        return [
            remote(
                row_send.at[turn], row_recv.at[turn, me_p], row_ss.at[turn, step], row_rs.at[turn, step],
                {"pipe": lax.rem(me_p + step, pipes), "seg": other_s},
            )
            for step in range(pipes)
        ]

    def send_duals(it):
        dual_recv[it, me_p] = dual[it]
        return [
            remote(
                dual.at[it], dual_recv.at[it, me_p], dual_ss.at[it, step], dual_rs.at[it, step],
                {"pipe": lax.rem(me_p + step, pipes)},
            )
            for step in range(1, pipes)
        ]

    def send_sums(it):
        return [
            remote(
                sum_send.at[it, lax.rem(me_p + step, pipes)], sum_recv.at[it, me_p],
                sum_ss.at[it, step], sum_rs.at[it, step],
                {"pipe": lax.rem(me_p + step, pipes)},
            )
            for step in range(1, pipes)
        ]

    def norm_copy(it, step):
        return pltpu.make_async_remote_copy(
            src_ref=norm_send.at[it], dst_ref=norm_recv.at[it, me],
            send_sem=norm_ss.at[it, step], recv_sem=norm_rs.at[it, step],
            device_id=peer(step), device_id_type=pl.DeviceIdType.MESH,
        )

    def fill_dual_rows(it, turn):
        for h in range(H):
            row_send[turn, h : h + 1, :] = mass[it, h, 0:1, :]
            row_send[turn, H + h : H + h + 1, :] = mom[it, h, S - 1 : S, :]

    def send_dual_halo(it, turn):
        rows = send_rows(turn)
        layer = remote(
            mass.at[it, 0], hour_recv.at[turn], hour_ss.at[turn], hour_rs.at[turn],
            {"hour": lax.rem(me_h + hours - 1, hours)},
        )
        return rows + [layer]

    get_mass.wait()
    get_mom.wait()
    fill_dual_rows(0, 0)
    get_dual.wait()
    pl.semaphore_wait(barrier, peers - 1)
    waiting_duals = send_duals(0)
    waiting_halo = send_dual_halo(0, 0)

    get_map.wait()
    start = pl.multiple_of(me_p * W, LANES)
    own_map = cmap[:, pl.ds(start, W)]
    class_rows = lax.broadcasted_iota(jnp.int32, (C, W), 0)
    for h in range(H):
        onehot_c[h] = jnp.where(own_map[h : h + 1, :] == class_rows, 1.0, 0.0).astype(jnp.bfloat16)
    get_match.wait()

    @pl.when(first_half)
    def _():
        wanted = match[:, pl.ds(start, W)]
        rows = lax.broadcasted_iota(jnp.int32, (LANES, W), 0)
        for block in range(0, T, LANES):
            hit = wanted == rows + block
            onehot_m[block : block + LANES, :] = jnp.where(hit, 1.0, 0.0).astype(jnp.bfloat16)

    @pl.when(jnp.logical_not(first_half))
    def _():
        columns = lax.broadcasted_iota(jnp.int32, (LANES, W), 1).astype(jnp.float32)
        columns = columns + start.astype(jnp.float32)
        for block in range(0, T, LANES):
            line = match[:, block : block + LANES].astype(jnp.float32)
            upright = jnp.transpose(jnp.broadcast_to(line, (LANES, LANES)))
            hit = jnp.concatenate([upright] * (W // LANES), axis=1) == columns
            onehot_m[block : block + LANES, :] = jnp.where(hit, 1.0, 0.0).astype(jnp.bfloat16)

    get_class.wait()
    kinds = classes[...]
    level = jnp.zeros((S, W), jnp.float32)
    for kind in range(table_ref.shape[0]):
        level = jnp.where(kinds == kind, table_ref[kind], level)
    fric[...] = level

    def matched_rows(turn):
        line = jnp.concatenate([row_recv[turn, block] for block in range(pipes)], axis=1)
        found = jnp.dot(pieces_of(line), onehot_m[...], preferred_element_type=jnp.float32)
        return joined(found, 2 * H)

    seg_at = lax.broadcasted_iota(jnp.int32, (S, W), 0)
    top, bottom = seg_at == 0, seg_at == S - 1
    get_flow.wait()
    get_pack.wait()
    get_cost.wait()

    outgoing = []

    def put(index, source, place):
        copy = pltpu.make_async_copy(source, place, out_sem.at[index])
        copy.start()
        outgoing.append(copy)

    weight = None
    for it in range(ITERS):
        turn = 2 * it
        for copy in waiting_halo:
            copy.wait_recv()
        found = matched_rows(turn)
        near = row_recv[turn, me_p]
        next_row = jnp.where(first_half, near, found)
        before_row = jnp.where(first_half, 0.0, near)
        for copy in waiting_duals:
            copy.wait_recv()
        spreads = []
        for h in range(H):
            held = jnp.concatenate([dual_recv[it, block, h] for block in range(pipes)], axis=0)
            spreads.append(
                joined(jnp.dot(pieces_of(held), onehot_c[h], preferred_element_type=jnp.float32), S)
            )
        if it == 0:
            primal_step, dual_step = STEP_SCALE, STEP_SCALE
        else:
            weight = finish_norms(it - 1, weight)
            primal_step, dual_step = STEP_SCALE / weight, STEP_SCALE * weight
        primal_sq = jnp.zeros((S, W), jnp.float32)
        for h in range(H):
            m, r = mass[it, h], mom[it, h]
            later = mass[it, h + 1] if h < H - 1 else jnp.where(last_hour, 0.0, hour_recv[turn])
            next_seg = jnp.where(bottom, next_row[h : h + 1], pltpu.roll(m, S - 1, 0))
            before = jnp.where(top, before_row[H + h : H + h + 1], pltpu.roll(r, 1, 0))
            grad_flow = m - next_seg + fric[...] * r
            grad_pack = m - later - r + before + share * spreads[h]
            f, q = flow[it, h], pack[it, h]
            flow_next = jnp.clip(f - primal_step * (cost[h] - grad_flow), -FLOW_CAP, FLOW_CAP)
            pack_next = jnp.clip(q + primal_step * grad_pack, 0.0, PACK_CAP)
            flow[it + 1, h] = flow_next
            pack[it + 1, h] = pack_next
            fb, pb = 2.0 * flow_next - f, 2.0 * pack_next - q
            flow_bar[it, h] = fb
            pack_bar[it, h] = pb
            row_send[turn + 1, h : h + 1, :] = fb[S - 1 : S]
            row_send[turn + 1, H + h : H + h + 1, :] = pb[0:1]
            primal_sq = primal_sq + (flow_next - f) ** 2 + (pack_next - q) ** 2
            partial = joined(
                lax.dot_general(
                    pieces_of(pb), onehot_c[h], (((1,), (1,)), ((), ())),
                    preferred_element_type=jnp.float32,
                ),
                S,
            )
            for block in range(pipes):
                sum_send[it, block, h] = partial[block * R : (block + 1) * R]
        waiting_sums = send_sums(it)
        waiting_halo = send_rows(turn + 1)
        waiting_halo.append(
            remote(
                pack_bar.at[it, H - 1], hour_recv.at[turn + 1], hour_ss.at[turn + 1], hour_rs.at[turn + 1],
                {"hour": lax.rem(me_h + 1, hours)},
            )
        )
        if it == ITERS - 1:
            put(0, flow.at[ITERS], flow_out)
            put(1, pack.at[ITERS], pack_out)
        primal_block = folded(primal_sq)
        sum_recv[it, me_p] = sum_send[it, me_p]
        if it == 0:
            get_inj.wait()
            get_target.wait()
        for copy in waiting_halo:
            copy.wait_recv()
        found = matched_rows(turn + 1)
        near = row_recv[turn + 1, me_p]
        first_row = jnp.where(first_half, found, near)
        after_row = jnp.where(last_half, 0.0, near)
        dual_sq = jnp.zeros((S, W), jnp.float32)
        for h in range(H):
            fb, pb = flow_bar[it, h], pack_bar[it, h]
            m, r = mass[it, h], mom[it, h]
            earlier = pack_bar[it, h - 1] if h > 0 else jnp.where(first_hour, 0.0, hour_recv[turn + 1])
            upstream = jnp.where(top, first_row[h : h + 1], pltpu.roll(fb, 1, 0))
            after = jnp.where(bottom, after_row[H + h : H + h + 1], pltpu.roll(pb, S - 1, 0))
            mass_next = m + dual_step * (inj[h] - (pb - earlier + fb - upstream))
            mom_next = r - dual_step * (fric[...] * fb - (pb - after))
            mass[it + 1, h] = mass_next
            mom[it + 1, h] = mom_next
            dual_sq = dual_sq + (mass_next - m) ** 2 + (mom_next - r) ** 2
        if it < ITERS - 1:
            fill_dual_rows(it + 1, turn + 2)
            waiting_halo = send_dual_halo(it + 1, turn + 2)
        else:
            put(2, mass.at[ITERS], mass_out)
            put(3, mom.at[ITERS], mom_out)
        dual_block = folded(dual_sq)
        for copy in waiting_sums:
            copy.wait_recv()
        totals = sum_recv[it, 0]
        for block in range(1, pipes):
            totals = totals + sum_recv[it, block]
        held = dual[it]
        dual_next = held + dual_step * (target[...] - share * totals)
        dual[it + 1] = dual_next
        if it < ITERS - 1:
            waiting_duals = send_duals(it + 1)
        else:
            put(4, dual.at[ITERS], dual_out)
        change = (dual_next - held) ** 2
        lines = jnp.sum(change, axis=0)
        if R % 8 == 0:
            dual_block = dual_block + folded(lines)
        else:
            spot = lax.broadcasted_iota(jnp.int32, (8, C), 0) == 0
            dual_block = dual_block + jnp.where(spot, jnp.sum(lines, axis=0, keepdims=True), 0.0)
        upper = lax.broadcasted_iota(jnp.int32, (8, LANES), 0) < 4
        both = jnp.where(
            upper, primal_block + pltpu.roll(primal_block, 4, 0), dual_block + pltpu.roll(dual_block, 4, 0)
        )
        norm_send[it] = both
        norm_recv[it, me] = both
        each_peer(lambda step: norm_copy(it, step).start())

        def finish_norms(it, weight):
            each_peer(lambda step: norm_copy(it, step).wait_recv())
            total = jnp.sum(norm_recv[it], axis=0)
            primal = jnp.sum(jnp.where(upper, total, 0.0), axis=(0, 1), keepdims=True)
            dual_all = jnp.sum(jnp.where(upper, 0.0, total), axis=(0, 1), keepdims=True)
            ratio = jnp.sqrt((dual_all + NORM_EPS) / (primal + NORM_EPS))
            return jnp.sqrt(ratio if weight is None else weight * ratio)

    weight = finish_norms(ITERS - 1, weight)
    weight_out[0] = jnp.sum(weight)
    for copy in sent:
        copy.wait_send()
    for it in range(ITERS):
        each_peer(lambda step: norm_copy(it, step).wait_send())
    for copy in outgoing:
        copy.wait()


def on_device(
    segment_flow, linepack, mass_dual, momentum_dual, contract_dual, flow_cost, injection, contract_target,
    friction_table, friction_class, matching, contract_map,
):
    H, S, W = segment_flow.shape
    C = contract_dual.shape[3]
    R = contract_dual.shape[2]
    pipes, hours, segs = lax.axis_size("pipe"), lax.axis_size("hour"), lax.axis_size("seg")
    peers = pipes * hours * segs
    T = W * pipes
    f32, i32 = jnp.float32, jnp.int32
    anywhere = pl.BlockSpec(memory_space=pl.ANY)
    smem = pl.BlockSpec(memory_space=pltpu.SMEM)
    cells = jax.ShapeDtypeStruct((H, S, W), f32)
    turns = 2 * ITERS
    dma = pltpu.SemaphoreType.DMA
    outs = pl.pallas_call(
        functools.partial(kernel, (pipes, hours, segs, H, S, W, C, R, T)),
        out_shape=(cells,) * 4
        + (jax.ShapeDtypeStruct((H, R, C), f32), jax.ShapeDtypeStruct((1,), f32)),
        in_specs=[smem] + [anywhere] * 11,
        out_specs=(anywhere,) * 5 + (smem,),
        scratch_shapes=[
            pltpu.VMEM((ITERS + 1, H, S, W), f32),
            pltpu.VMEM((ITERS + 1, H, S, W), f32),
            pltpu.VMEM((ITERS + 1, H, S, W), f32),
            pltpu.VMEM((ITERS + 1, H, S, W), f32),
            pltpu.VMEM((ITERS + 1, H, R, C), f32),
            pltpu.VMEM((H, S, W), f32),
            pltpu.VMEM((H, S, W), f32),
            pltpu.VMEM((H, R, C), f32),
            pltpu.VMEM((S, W), i32),
            pltpu.VMEM((1, T), i32),
            pltpu.VMEM((H, T), i32),
            pltpu.VMEM((S, W), f32),
            pltpu.VMEM((ITERS, H, S, W), f32),
            pltpu.VMEM((ITERS, H, S, W), f32),
            pltpu.VMEM((H, C, W), jnp.bfloat16),
            pltpu.VMEM((T, W), jnp.bfloat16),
            pltpu.VMEM((turns, 2 * H, W), f32),
            pltpu.VMEM((turns, pipes, 2 * H, W), f32),
            pltpu.VMEM((turns, S, W), f32),
            pltpu.VMEM((ITERS, pipes, H, R, C), f32),
            pltpu.VMEM((ITERS, pipes, H, R, C), f32),
            pltpu.VMEM((ITERS, pipes, H, R, C), f32),
            pltpu.VMEM((ITERS, 8, LANES), f32),
            pltpu.VMEM((ITERS, peers, 8, LANES), f32),
            dma((11,)),
            dma((5,)),
            dma((turns, pipes)),
            dma((turns, pipes)),
            dma((turns,)),
            dma((turns,)),
            dma((ITERS, pipes)),
            dma((ITERS, pipes)),
            dma((ITERS, pipes)),
            dma((ITERS, pipes)),
            dma((ITERS, peers)),
            dma((ITERS, peers)),
        ],
        compiler_params=pltpu.CompilerParams(
            collective_id=0, has_side_effects=True, vmem_limit_bytes=48 * 1024 * 1024
        ),
        cost_estimate=pl.CostEstimate(flops=10**8, bytes_accessed=2 * 10**6, transcendentals=0),
    )(
        friction_table, segment_flow, linepack, mass_dual, momentum_dual, contract_dual.reshape(H, R, C),
        flow_cost, injection, contract_target.reshape(H, R, C), friction_class, matching.reshape(1, T),
        contract_map,
    )
    return outs[:4] + (outs[4].reshape(contract_dual.shape), outs[5])


def solution(mesh):
    cells = P(("groups", "hour"), "seg", "pipe")
    contracts = P(("groups", "hour"), "seg", "pipe", None)
    return jax.shard_map(
        on_device,
        mesh=mesh,
        in_specs=(
            cells, cells, cells, cells, contracts, cells, cells, contracts,
            P(), P("seg", ("groups", "pipe")), P("groups"), P(("groups", "hour"), None),
        ),
        out_specs=(cells, cells, cells, cells, contracts, P("groups")),
        check_vma=False,
    )
```

time: 257 us -> 49 us (0.19)
  blocking collectives: 123 us -> 0 us
  starting transfers between devices: 57.3 us -> 0 us
  Pallas kernels: 0 us -> 33.8 us
  local copies, waits for them, and re-layouts: 34.9 us -> 12.2 us
  other arithmetic: 15.8 us -> 0 us
  between operations: 12.1 us -> 2.44 us
  matrix products: 8.66 us -> 0 us
  waiting for transfers between devices: 3.97 us -> 0 us
    psum x2 -> x0, blocking collectives: 65.5 us -> none  [on_device(): lax.psum((primal_sq, dual_sq), ('pipe', 'hour', 'seg'))]
    all_gather x4 -> x0, blocking collectives: 57.8 us -> none  [other_half(): lax.all_gather(edge_row[:, None, :], ('pipe', 'seg'), axis=1, tiled=True)]
    ppermute x16 -> x0, starting transfers between devices: 38.5 us -> none  [the longest x8 27.9 us: padded(): lax.ppermute(tail, axis, [(i, (i + 1) % count) for i in range(ends)])]
    pallas_call x0 -> x1, Pallas kernels: none -> 33.8 us  [on_device(): pl.pallas_call(functools.partial(kernel, (pipes, hours, segs, H, S, W, C,...]
    all_to_all x4 -> x0, starting transfers between devices: 18.8 us -> none  [the longest x2 10.8 us: on_device(): lax.all_to_all(hour_spread, 'pipe', split_axis=2, concat_axis=1, tiled=True)]
    dot_general x4 -> x0, matrix products: 8.66 us -> none  [the longest x2 4.64 us: add_block(): jnp.einsum('hsp,hpc->hsc', partial_value, onehot, precision=lax.Precision...]
    reduce_sum x5 -> x0, other arithmetic: 6.1 us -> none  [the longest x2 2.16 us: on_device(): jnp.sum((pack_next - linepack) ** 2)]
    unnamed x55 -> x29, local copies, waits for them, and re-layouts: 17 us -> 12.2 us
  transfers between devices with their start and end apart: 20 -> 0, of which waited for: 3 -> 0; matrix products, arithmetic and copies ran while one was open for 16% -> 0% of each run, Pallas kernels for 0% -> 0%
where the time goes in v1:
time: 49 us; the launch traced here: 48.5 us
  Pallas kernels  33.8 us (69%)
  local copies, waits for them, and re-layouts  12.2 us (25%)
  between operations  2.44 us (5%)
    pallas_call x1, Pallas kernels, on_device(): pl.pallas_call(functools.partial(kernel, (pipes, hours, segs, H, S, W, C,...  33.8 us
    unnamed x29, local copies, waits for them, and re-layouts  12.2 us

profile of v1, /device:TPU:0, one launch (start us, length us, event | category | flops | bytes accessed | tf_op | source)
XLA Modules:
  0.0 48.5 jit_solution(9533084952318144952)
XLA Ops:
  0.6 0.0 copy-start.10
  0.6 0.0 copy-start.11
  0.7 0.7 %copy-done.10 = s32[1024]{0:T(1024)S(1)} copy-done((s32[1024]{0:T(1024)S(1)}, s32[1024]{0:T(1024)}, u32[]{:S(2)}) %copy-start.10) | copy-done | bytes 4120
  1.3 0.0 copy-done.11
  1.3 0.0 copy-start
  1.3 0.9 %copy-done = f32[4,32,256]{2,1,0:T(8,128)S(1)} copy-done((f32[4,32,256]{2,1,0:T(8,128)S(1)}, f32[4,32,256]{2,1,0:T(8,128)}, u32[]{:S(2)}) %copy-start) | copy-done | bytes 131096
  2.2 0.0 copy-start.1
  2.2 0.9 %copy-done.1 = f32[4,32,256]{2,1,0:T(8,128)S(1)} copy-done((f32[4,32,256]{2,1,0:T(8,128)S(1)}, f32[4,32,256]{2,1,0:T(8,128)}, u32[]{:S(2)}) %copy-start.1) | copy-done | bytes 131096
  3.1 0.0 copy-start.2
  3.1 0.9 %copy-done.2 = f32[4,32,256]{2,1,0:T(8,128)S(1)} copy-done((f32[4,32,256]{2,1,0:T(8,128)S(1)}, f32[4,32,256]{2,1,0:T(8,128)}, u32[]{:S(2)}) %copy-start.2) | copy-done | bytes 131096
  4.0 0.0 copy-start.3
  4.0 0.9 %copy-done.3 = f32[4,32,256]{2,1,0:T(8,128)S(1)} copy-done((f32[4,32,256]{2,1,0:T(8,128)S(1)}, f32[4,32,256]{2,1,0:T(8,128)}, u32[]{:S(2)}) %copy-start.3) | copy-done | bytes 131096
  4.9 0.0 copy-start.4
  5.0 0.9 %copy-done.4 = f32[4,32,256]{2,1,0:T(8,128)S(1)} copy-done((f32[4,32,256]{2,1,0:T(8,128)S(1)}, f32[4,32,256]{2,1,0:T(8,128)}, u32[]{:S(2)}) %copy-start.4) | copy-done | bytes 131096
  5.9 0.0 copy-start.5
  5.9 0.9 %copy-done.5 = f32[4,32,256]{2,1,0:T(8,128)S(1)} copy-done((f32[4,32,256]{2,1,0:T(8,128)S(1)}, f32[4,32,256]{2,1,0:T(8,128)}, u32[]{:S(2)}) %copy-start.5) | copy-done | bytes 131096
  6.8 0.0 copy-start.6
  6.8 0.8 %copy-done.6 = s32[32,256]{1,0:T(8,128)S(1)} copy-done((s32[32,256]{1,0:T(8,128)S(1)}, s32[32,256]{1,0:T(8,128)}, u32[]{:S(2)}) %copy-start.6) | copy-done | bytes 32792
  7.5 0.0 copy-start.7
  7.5 0.7 %copy-done.7 = f32[4,1,8,128]{3,2,1,0:T(8,128)S(1)} copy-done((f32[4,1,8,128]{3,2,1,0:T(8,128)S(1)}, f32[4,1,8,128]{3,2,1,0:T(8,128)}, u32[]{:S(2)}) %copy-start.7) | copy-done | bytes 16408
  8.2 0.0 copy-start.8
  8.2 0.7 %copy-done.8 = f32[4,1,8,128]{3,2,1,0:T(8,128)S(1)} copy-done((f32[4,1,8,128]{3,2,1,0:T(8,128)S(1)}, f32[4,1,8,128]{3,2,1,0:T(8,128)}, u32[]{:S(2)}) %copy-start.8) | copy-done | bytes 16408
  9.0 0.0 copy-start.9
  9.0 0.7 %copy-done.9 = s32[4,1024]{1,0:T(4,128)S(1)} copy-done((s32[4,1024]{1,0:T(4,128)S(1)}, s32[4,1024]{1,0:T(4,128)}, u32[]{:S(2)}) %copy-start.9) | copy-done | bytes 16408
  9.7 33.8 %shard_map.163 = (f32[4,32,256]{2,1,0:T(8,128)S(1)}, f32[4,32,256]{2,1,0:T(8,128)S(1)}, f32[4,32,256]{2,1,0:T(8,128)S(1)}, f32[4,32,256]{2,1,0:T(8,128)S(1)}, f32[4,8,128]{2,1,0:T(8,128)S(1)}, /*index=5*/f32[1]{0:T(128)}) custom-call(f32[16]{0:T(128)S(1)} %copy-done.11, f32[4,32,256]{2,1,0:T(8,128)S(1)} %copy-done, f32[4,32,256]{2,1,0:T(8,128)S(1)} %copy-done.1, ...), custom_call_target="tpu_custom_call" | custom-call | flops 100000000 | bytes 2000000 | tf_op jit(solution)/shard_map/pallas_call | solution.py:378
  43.5 0.7 %copy.25 = f32[4,32,256]{2,1,0:T(8,128)} copy(f32[4,32,256]{2,1,0:T(8,128)S(1)} %get-tuple-element.30) | data formatting | bytes 262144
  44.2 0.7 %copy.26 = f32[4,32,256]{2,1,0:T(8,128)} copy(f32[4,32,256]{2,1,0:T(8,128)S(1)} %get-tuple-element.31) | data formatting | bytes 262144
  44.8 0.7 %copy.27 = f32[4,32,256]{2,1,0:T(8,128)} copy(f32[4,32,256]{2,1,0:T(8,128)S(1)} %get-tuple-element.32) | data formatting | bytes 262144
  45.5 0.7 %copy.28 = f32[4,32,256]{2,1,0:T(8,128)} copy(f32[4,32,256]{2,1,0:T(8,128)S(1)} %get-tuple-element.33) | data formatting | bytes 262144
  46.1 0.6 %copy.29 = f32[4,1,8,128]{3,2,1,0:T(8,128)} copy(f32[4,1,8,128]{3,2,1,0:T(8,128)S(1)} %bitcast.8) | data formatting | bytes 32768
Async XLA Ops:
  0.6 0.7 %copy-start.10 = (s32[1024]{0:T(1024)S(1)}, s32[1024]{0:T(1024)}, u32[]{:S(2)}) copy-start(s32[1024]{0:T(1024)} %param.22) | copy-start | bytes 12292
  0.6 0.7 %copy-start.11 = (f32[16]{0:T(128)S(1)}, f32[16]{0:T(128)}, u32[]{:S(2)}) copy-start(f32[16]{0:T(128)} %table_ref.1) | copy-start | bytes 196
  1.3 0.9 %copy-start = (f32[4,32,256]{2,1,0:T(8,128)S(1)}, f32[4,32,256]{2,1,0:T(8,128)}, u32[]{:S(2)}) copy-start(f32[4,32,256]{2,1,0:T(8,128)} %flow_in.1) | copy-start | bytes 393220
  2.2 0.9 %copy-start.1 = (f32[4,32,256]{2,1,0:T(8,128)S(1)}, f32[4,32,256]{2,1,0:T(8,128)}, u32[]{:S(2)}) copy-start(f32[4,32,256]{2,1,0:T(8,128)} %pack_in.1) | copy-start | bytes 393220
  3.1 0.9 %copy-start.2 = (f32[4,32,256]{2,1,0:T(8,128)S(1)}, f32[4,32,256]{2,1,0:T(8,128)}, u32[]{:S(2)}) copy-start(f32[4,32,256]{2,1,0:T(8,128)} %mass_in.1) | copy-start | bytes 393220
  4.0 0.9 %copy-start.3 = (f32[4,32,256]{2,1,0:T(8,128)S(1)}, f32[4,32,256]{2,1,0:T(8,128)}, u32[]{:S(2)}) copy-start(f32[4,32,256]{2,1,0:T(8,128)} %mom_in.1) | copy-start | bytes 393220
  4.9 0.9 %copy-start.4 = (f32[4,32,256]{2,1,0:T(8,128)S(1)}, f32[4,32,256]{2,1,0:T(8,128)}, u32[]{:S(2)}) copy-start(f32[4,32,256]{2,1,0:T(8,128)} %cost_in.1) | copy-start | bytes 393220
  5.9 0.9 %copy-start.5 = (f32[4,32,256]{2,1,0:T(8,128)S(1)}, f32[4,32,256]{2,1,0:T(8,128)}, u32[]{:S(2)}) copy-start(f32[4,32,256]{2,1,0:T(8,128)} %inj_in.1) | copy-start | bytes 393220
  6.8 0.8 %copy-start.6 = (s32[32,256]{1,0:T(8,128)S(1)}, s32[32,256]{1,0:T(8,128)}, u32[]{:S(2)}) copy-start(s32[32,256]{1,0:T(8,128)} %class_in.1) | copy-start | bytes 98308
  7.5 0.7 %copy-start.7 = (f32[4,1,8,128]{3,2,1,0:T(8,128)S(1)}, f32[4,1,8,128]{3,2,1,0:T(8,128)}, u32[]{:S(2)}) copy-start(f32[4,1,8,128]{3,2,1,0:T(8,128)} %param.16) | copy-start | bytes 49156
  8.2 0.7 %copy-start.8 = (f32[4,1,8,128]{3,2,1,0:T(8,128)S(1)}, f32[4,1,8,128]{3,2,1,0:T(8,128)}, u32[]{:S(2)}) copy-start(f32[4,1,8,128]{3,2,1,0:T(8,128)} %param.19) | copy-start | bytes 49156
  9.0 0.7 %copy-start.9 = (s32[4,1024]{1,0:T(4,128)S(1)}, s32[4,1024]{1,0:T(4,128)}, u32[]{:S(2)}) copy-start(s32[4,1024]{1,0:T(4,128)} %map_in.1) | copy-start | bytes 49156

commit v2 on v1

--- a/solution.py
+++ b/solution.py
@@ -359,6 +359,16 @@
         copy.wait()
 
 
+def store_kernel(*refs):
+    count = (len(refs) - 1) // 2
+    sem = refs[-1]
+    copies = [pltpu.make_async_copy(refs[i], refs[count + i], sem.at[i]) for i in range(count)]
+    for copy in copies:
+        copy.start()
+    for copy in copies:
+        copy.wait()
+
+
 def on_device(
     segment_flow, linepack, mass_dual, momentum_dual, contract_dual, flow_cost, injection, contract_target,
     friction_table, friction_class, matching, contract_map,
@@ -371,6 +381,7 @@
     T = W * pipes
     f32, i32 = jnp.float32, jnp.int32
     anywhere = pl.BlockSpec(memory_space=pl.ANY)
+    hbm = pl.BlockSpec(memory_space=pltpu.HBM)
     smem = pl.BlockSpec(memory_space=pltpu.SMEM)
     cells = jax.ShapeDtypeStruct((H, S, W), f32)
     turns = 2 * ITERS
@@ -379,7 +390,7 @@
         functools.partial(kernel, (pipes, hours, segs, H, S, W, C, R, T)),
         out_shape=(cells,) * 4
         + (jax.ShapeDtypeStruct((H, R, C), f32), jax.ShapeDtypeStruct((1,), f32)),
-        in_specs=[smem] + [anywhere] * 11,
+        in_specs=[smem] + [hbm] * 11,
         out_specs=(anywhere,) * 5 + (smem,),
         scratch_shapes=[
             pltpu.VMEM((ITERS + 1, H, S, W), f32),
@@ -420,7 +431,7 @@
             dma((ITERS, peers)),
         ],
         compiler_params=pltpu.CompilerParams(
-            collective_id=0, has_side_effects=True, vmem_limit_bytes=48 * 1024 * 1024
+            collective_id=0, has_side_effects=True, vmem_limit_bytes=63 * 1024 * 1024
         ),
         cost_estimate=pl.CostEstimate(flops=10**8, bytes_accessed=2 * 10**6, transcendentals=0),
     )(
@@ -428,7 +439,14 @@
         flow_cost, injection, contract_target.reshape(H, R, C), friction_class, matching.reshape(1, T),
         contract_map,
     )
-    return outs[:4] + (outs[4].reshape(contract_dual.shape), outs[5])
+    stored = pl.pallas_call(
+        store_kernel,
+        out_shape=(cells,) * 4 + (jax.ShapeDtypeStruct((H, R, C), f32),),
+        in_specs=[anywhere] * 5,
+        out_specs=(hbm,) * 5,
+        scratch_shapes=[dma((5,))],
+    )(*outs[:5])
+    return tuple(stored[:4]) + (stored[4].reshape(contract_dual.shape), outs[5])
 
 
 def solution(mesh):

time: 49 us -> 52.5 us (1.071)
  Pallas kernels: 33.8 us -> 49.9 us
  local copies, waits for them, and re-layouts: 12.2 us -> 0 us
    pallas_call x0 -> x1, Pallas kernels: none -> 17.5 us  [on_device(): pl.pallas_call(store_kernel, out_shape=(cells,) * 4 + (jax.ShapeDtypeStru...]
    unnamed x29 -> x0, local copies, waits for them, and re-layouts: 12.2 us -> none
    pallas_call x1, Pallas kernels: 33.8 us -> 32.4 us  [on_device(): pl.pallas_call(functools.partial(kernel, (pipes, hours, segs, H, S, W, C,...]
where the time goes in v2:
time: 52.5 us; the launch traced here: 52.3 us
  Pallas kernels  49.9 us (95%)
  between operations  2.38 us (5%)
    pallas_call x1, Pallas kernels, on_device(): pl.pallas_call(functools.partial(kernel, (pipes, hours, segs, H, S, W, C,...  32.4 us
    pallas_call x1, Pallas kernels, on_device(): pl.pallas_call(store_kernel, out_shape=(cells,) * 4 + (jax.ShapeDtypeStru...  17.5 us

profile of v2, /device:TPU:0, one launch (start us, length us, event | category | flops | bytes accessed | tf_op | source)
XLA Modules:
  0.0 52.3 jit_solution(16971982952889218198)
XLA Ops:
  0.6 32.4 %shard_map.163 = (f32[4,32,256]{2,1,0:T(8,128)}, f32[4,32,256]{2,1,0:T(8,128)}, f32[4,32,256]{2,1,0:T(8,128)}, f32[4,32,256]{2,1,0:T(8,128)}, f32[4,8,128]{2,1,0:T(8,128)}, /*index=5*/f32[1]{0:T(128)}) custom-call(f32[16]{0:T(128)} %table_ref.1, f32[4,32,256]{2,1,0:T(8,128)} %flow_in.1, f32[4,32,256]{2,1,0:T(8,128)} %pack_in.1, f32[4,32,256]{2,1,0:T(8,128)} %mass_in.1, ...), custom_call_target="tpu_custom_call" | custom-call | flops 100000000 | bytes 2000000 | tf_op jit(solution)/shard_map/pallas_call | solution.py:389
  33.0 17.5 %shard_map.164 = (f32[4,32,256]{2,1,0:T(8,128)}, f32[4,32,256]{2,1,0:T(8,128)}, f32[4,32,256]{2,1,0:T(8,128)}, f32[4,32,256]{2,1,0:T(8,128)}, f32[4,8,128]{2,1,0:T(8,128)}) custom-call(f32[4,32,256]{2,1,0:T(8,128)} %get-tuple-element.17.refs_0_, f32[4,32,256]{2,1,0:T(8,128)} %get-tuple-element.18.refs_1_, f32[4,32,256]{2,1,0:T(8,128)} %get-tuple-element.19.refs_2_, ...), custom_call_target="tpu_custom_call" | custom-call | tf_op jit(solution)/shard_map/pallas_call | solution.py:442

commit v3 on v2

--- a/solution.py
+++ b/solution.py
@@ -360,12 +360,17 @@
 
 
 def store_kernel(*refs):
-    count = (len(refs) - 1) // 2
-    sem = refs[-1]
-    copies = [pltpu.make_async_copy(refs[i], refs[count + i], sem.at[i]) for i in range(count)]
-    for copy in copies:
+    count = (len(refs) - 2) // 3
+    sources, places, held = refs[:count], refs[count : 2 * count], refs[2 * count : 3 * count]
+    in_sem, out_sem = refs[-2:]
+    loads = [pltpu.make_async_copy(sources[i], held[i], in_sem.at[i]) for i in range(count)]
+    stores = [pltpu.make_async_copy(held[i], places[i], out_sem.at[i]) for i in range(count)]
+    for copy in loads:
         copy.start()
-    for copy in copies:
+    for load, store in zip(loads, stores):
+        load.wait()
+        store.start()
+    for copy in stores:
         copy.wait()
 
 
@@ -444,7 +449,9 @@
         out_shape=(cells,) * 4 + (jax.ShapeDtypeStruct((H, R, C), f32),),
         in_specs=[anywhere] * 5,
         out_specs=(hbm,) * 5,
-        scratch_shapes=[dma((5,))],
+        scratch_shapes=[pltpu.VMEM((H, S, W), f32)] * 4
+        + [pltpu.VMEM((H, R, C), f32), dma((5,)), dma((5,))],
+        compiler_params=pltpu.CompilerParams(vmem_limit_bytes=63 * 1024 * 1024),
     )(*outs[:5])
     return tuple(stored[:4]) + (stored[4].reshape(contract_dual.shape), outs[5])
 

time: 52.5 us -> 36.8 us (0.70)
  Pallas kernels: 49.9 us -> 34.2 us
    pallas_call x1, Pallas kernels: 17.5 us -> 1.84 us  [on_device(): pl.pallas_call(store_kernel, out_shape=(cells,) * 4 + (jax.ShapeDtypeStru...]
where the time goes in v3:
time: 36.8 us; the launch traced here: 36.6 us
  Pallas kernels  34.2 us (93%)
  between operations  2.38 us (6%)
    pallas_call x1, Pallas kernels, on_device(): pl.pallas_call(functools.partial(kernel, (pipes, hours, segs, H, S, W, C,...  32.4 us
    pallas_call x1, Pallas kernels, on_device(): pl.pallas_call(store_kernel, out_shape=(cells,) * 4 + (jax.ShapeDtypeStru...  1.84 us

profile of v3, /device:TPU:0, one launch (start us, length us, event | category | flops | bytes accessed | tf_op | source)
XLA Modules:
  0.0 36.6 jit_solution(8487785508395735855)
XLA Ops:
  0.6 32.4 %shard_map.163 = (f32[4,32,256]{2,1,0:T(8,128)}, f32[4,32,256]{2,1,0:T(8,128)}, f32[4,32,256]{2,1,0:T(8,128)}, f32[4,32,256]{2,1,0:T(8,128)}, f32[4,8,128]{2,1,0:T(8,128)}, /*index=5*/f32[1]{0:T(128)}) custom-call(f32[16]{0:T(128)} %table_ref.1, f32[4,32,256]{2,1,0:T(8,128)} %flow_in.1, f32[4,32,256]{2,1,0:T(8,128)} %pack_in.1, f32[4,32,256]{2,1,0:T(8,128)} %mass_in.1, ...), custom_call_target="tpu_custom_call" | custom-call | flops 100000000 | bytes 2000000 | tf_op jit(solution)/shard_map/pallas_call | solution.py:394
  33.0 1.8 %shard_map.164 = (f32[4,32,256]{2,1,0:T(8,128)}, f32[4,32,256]{2,1,0:T(8,128)}, f32[4,32,256]{2,1,0:T(8,128)}, f32[4,32,256]{2,1,0:T(8,128)}, f32[4,8,128]{2,1,0:T(8,128)}) custom-call(f32[4,32,256]{2,1,0:T(8,128)} %get-tuple-element.17.refs_0_, f32[4,32,256]{2,1,0:T(8,128)} %get-tuple-element.18.refs_1_, f32[4,32,256]{2,1,0:T(8,128)} %get-tuple-element.19.refs_2_, ...), custom_call_target="tpu_custom_call" | custom-call | tf_op jit(solution)/shard_map/pallas_call | solution.py:447

commit v4 on v3

--- a/solution.py
+++ b/solution.py
@@ -13,7 +13,7 @@
 STEP_SCALE = 0.25
 NORM_EPS = 1e-06
 LANES = 128
-PIECES = 3
+PIECES = 2
 
 
 def pieces_of(values):

time: 36.8 us -> 36.7 us (level)
  no operation moved by 1% of the time
where the time goes in v4:
time: 36.7 us; the launch traced here: 36.5 us
  Pallas kernels  34.1 us (93%)
  between operations  2.38 us (6%)
    pallas_call x1, Pallas kernels, on_device(): pl.pallas_call(functools.partial(kernel, (pipes, hours, segs, H, S, W, C,...  32.3 us
    pallas_call x1, Pallas kernels, on_device(): pl.pallas_call(store_kernel, out_shape=(cells,) * 4 + (jax.ShapeDtypeStru...  1.84 us

profile of v4, /device:TPU:0, one launch (start us, length us, event | category | flops | bytes accessed | tf_op | source)
XLA Modules:
  0.0 36.5 jit_solution(3254683951518272256)
XLA Ops:
  0.6 32.3 %shard_map.163 = (f32[4,32,256]{2,1,0:T(8,128)}, f32[4,32,256]{2,1,0:T(8,128)}, f32[4,32,256]{2,1,0:T(8,128)}, f32[4,32,256]{2,1,0:T(8,128)}, f32[4,8,128]{2,1,0:T(8,128)}, /*index=5*/f32[1]{0:T(128)}) custom-call(f32[16]{0:T(128)} %table_ref.1, f32[4,32,256]{2,1,0:T(8,128)} %flow_in.1, f32[4,32,256]{2,1,0:T(8,128)} %pack_in.1, f32[4,32,256]{2,1,0:T(8,128)} %mass_in.1, ...), custom_call_target="tpu_custom_call" | custom-call | flops 100000000 | bytes 2000000 | tf_op jit(solution)/shard_map/pallas_call | solution.py:394
  32.9 1.8 %shard_map.164 = (f32[4,32,256]{2,1,0:T(8,128)}, f32[4,32,256]{2,1,0:T(8,128)}, f32[4,32,256]{2,1,0:T(8,128)}, f32[4,32,256]{2,1,0:T(8,128)}, f32[4,8,128]{2,1,0:T(8,128)}) custom-call(f32[4,32,256]{2,1,0:T(8,128)} %get-tuple-element.17.refs_0_, f32[4,32,256]{2,1,0:T(8,128)} %get-tuple-element.18.refs_1_, f32[4,32,256]{2,1,0:T(8,128)} %get-tuple-element.19.refs_2_, ...), custom_call_target="tpu_custom_call" | custom-call | tf_op jit(solution)/shard_map/pallas_call | solution.py:447

commit v5 on v3

--- a/solution.py
+++ b/solution.py
@@ -168,16 +168,22 @@
     get_mom.wait()
     fill_dual_rows(0, 0)
     get_dual.wait()
-    pl.semaphore_wait(barrier, peers - 1)
-    waiting_duals = send_duals(0)
-    waiting_halo = send_dual_halo(0, 0)
-
     get_map.wait()
     start = pl.multiple_of(me_p * W, LANES)
     own_map = cmap[:, pl.ds(start, W)]
     class_rows = lax.broadcasted_iota(jnp.int32, (C, W), 0)
     for h in range(H):
         onehot_c[h] = jnp.where(own_map[h : h + 1, :] == class_rows, 1.0, 0.0).astype(jnp.bfloat16)
+    get_class.wait()
+    kinds = classes[...]
+    level = jnp.zeros((S, W), jnp.float32)
+    for kind in range(table_ref.shape[0]):
+        level = jnp.where(kinds == kind, table_ref[kind], level)
+    fric[...] = level
+    pl.semaphore_wait(barrier, peers - 1)
+    waiting_duals = send_duals(0)
+    waiting_halo = send_dual_halo(0, 0)
+
     get_match.wait()
 
     @pl.when(first_half)
@@ -197,13 +203,6 @@
             upright = jnp.transpose(jnp.broadcast_to(line, (LANES, LANES)))
             hit = jnp.concatenate([upright] * (W // LANES), axis=1) == columns
             onehot_m[block : block + LANES, :] = jnp.where(hit, 1.0, 0.0).astype(jnp.bfloat16)
-
-    get_class.wait()
-    kinds = classes[...]
-    level = jnp.zeros((S, W), jnp.float32)
-    for kind in range(table_ref.shape[0]):
-        level = jnp.where(kinds == kind, table_ref[kind], level)
-    fric[...] = level
 
     def matched_rows(turn):
         line = jnp.concatenate([row_recv[turn, block] for block in range(pipes)], axis=1)

time: 36.8 us -> 36.8 us (level)
  no operation moved by 1% of the time
where the time goes in v5:
time: 36.8 us; the launch traced here: 36.6 us
  Pallas kernels  34.2 us (93%)
  between operations  2.38 us (6%)
    pallas_call x1, Pallas kernels, on_device(): pl.pallas_call(functools.partial(kernel, (pipes, hours, segs, H, S, W, C,...  32.4 us
    pallas_call x1, Pallas kernels, on_device(): pl.pallas_call(store_kernel, out_shape=(cells,) * 4 + (jax.ShapeDtypeStru...  1.84 us

profile of v5, /device:TPU:0, one launch (start us, length us, event | category | flops | bytes accessed | tf_op | source)
XLA Modules:
  0.0 36.6 jit_solution(15421857563826538605)
XLA Ops:
  0.6 32.4 %shard_map.163 = (f32[4,32,256]{2,1,0:T(8,128)}, f32[4,32,256]{2,1,0:T(8,128)}, f32[4,32,256]{2,1,0:T(8,128)}, f32[4,32,256]{2,1,0:T(8,128)}, f32[4,8,128]{2,1,0:T(8,128)}, /*index=5*/f32[1]{0:T(128)}) custom-call(f32[16]{0:T(128)} %table_ref.1, f32[4,32,256]{2,1,0:T(8,128)} %flow_in.1, f32[4,32,256]{2,1,0:T(8,128)} %pack_in.1, f32[4,32,256]{2,1,0:T(8,128)} %mass_in.1, ...), custom_call_target="tpu_custom_call" | custom-call | flops 100000000 | bytes 2000000 | tf_op jit(solution)/shard_map/pallas_call | solution.py:393
  33.1 1.8 %shard_map.164 = (f32[4,32,256]{2,1,0:T(8,128)}, f32[4,32,256]{2,1,0:T(8,128)}, f32[4,32,256]{2,1,0:T(8,128)}, f32[4,32,256]{2,1,0:T(8,128)}, f32[4,8,128]{2,1,0:T(8,128)}) custom-call(f32[4,32,256]{2,1,0:T(8,128)} %get-tuple-element.17.refs_0_, f32[4,32,256]{2,1,0:T(8,128)} %get-tuple-element.18.refs_1_, f32[4,32,256]{2,1,0:T(8,128)} %get-tuple-element.19.refs_2_, ...), custom_call_target="tpu_custom_call" | custom-call | tf_op jit(solution)/shard_map/pallas_call | solution.py:446
